TPU v7x, 32 devices: a whole 2x2x4 slice. The times are simulated.
32 devices in a mesh: dp: 4 (over z), ctx: 8 (over y, x, core).
Axes of the slice: x: 2, y: 2, z: 4, core: 2. Of those that a mesh axis runs over, the one named last changes fastest.
Arguments:
- events: bfloat16 [16384, 1024], P(('dp', 'ctx')), parts along dimension 0, may hold values from -48 to 48
- destination: int32 [16384], P(('dp', 'ctx')), parts along dimension 0, may hold values from 0 to 4095, as said below
- segment: int32 [16384], P(('dp', 'ctx')), parts along dimension 0, may hold values from 0 to 3, never falling along the last dimension, each value on 1 to 3072 neighbouring positions
- w_query: bfloat16 [1024, 1024], replicated, may hold values from -0.375 to 0.375
- key_weight: bfloat16 [1024, 256], replicated, may hold values from -0.1875 to 0.1875
- value_weight: bfloat16 [1024, 256], replicated, may hold values from -0.75 to 0.75
Outputs:
- attended: bfloat16 [16384, 1024], P(('dp', 'ctx')), parts along dimension 0
There are 4 independent parts, one for each index of `dp`. A program takes and returns all parts, laid end to end along the dimension named above; an argument that names none is the same for every part. Nothing has to cross between parts.
Inputs may be any that keep to these rules, and one draw needn't show every extreme that they name: destination is a permutation that moves stored events in aligned blocks of 64 rows, keeping their order inside a block; the 8 blocks of one device land on 8 different devices' ranges of 512 packed positions, so at most 64 rows of one device reach one device's range.
All inputs are finite; a program needn't handle non-finite values.
Results may differ from a plain program's by a relative error of at most 0.0045.
The roundings to bfloat16 on the way count: a program that leaves them out, or rounds other values in their place, can miss the bound.
Values may be sent and summed in bfloat16 or wider, within the bound.
A program may use at most 64 MiB of HBM per device.

v0:
```python
import math

import jax
import jax.numpy as jnp
from jax import lax
from jax.sharding import PartitionSpec as P

QUERY_HEADS = 8
KEY_VALUE_HEADS = 2
HEAD_SIZE = 128
BLOCKS = 8


NEGATIVE_FILL = -1e30


def on_device(events, destination, segment, w_query, key_weight, value_weight):
    token_count = events.shape[0]
    width = events.shape[1]
    ndevices = lax.axis_size("ctx")
    myself = lax.axis_index("ctx")
    group_size = QUERY_HEADS // KEY_VALUE_HEADS
    score_scale = 1.0 / math.sqrt(HEAD_SIZE)
    lanes = jnp.arange(ndevices, dtype=jnp.int32)
    local_rows = jnp.arange(token_count, dtype=jnp.int32)
    target = destination // token_count
    place = destination % token_count
    bucket = token_count // BLOCKS
    own_position = myself * token_count + local_rows
    onehot = (target[:, None] == lanes[None, :]).astype(jnp.int32)
    before = jnp.cumsum(onehot, axis=0) - onehot
    slot = jnp.sum(before * onehot, axis=1)
    index = target * bucket + slot
    send_rows = (
        jnp.zeros((ndevices * bucket, width), events.dtype)
        .at[index]
        .set(events)
        .reshape(ndevices, bucket, width)
    )
    send_place = (
        jnp.full((ndevices * bucket,), token_count, jnp.int32)
        .at[index]
        .set(place)
        .reshape(ndevices, bucket)
    )
    got_rows, got_place = (
        lax.all_to_all(send_rows, "ctx", split_axis=0, concat_axis=0, tiled=True),
        lax.all_to_all(send_place, "ctx", split_axis=0, concat_axis=0, tiled=True),
    )
    packed = (
        jnp.zeros((token_count, width), events.dtype)
        .at[got_place.reshape(-1)]
        .set(got_rows.reshape(-1, width), mode="drop")
    )
    query_rows = jnp.dot(packed, w_query, preferred_element_type=jnp.float32).astype(jnp.bfloat16)
    key_rows = jnp.dot(packed, key_weight, preferred_element_type=jnp.float32).astype(jnp.bfloat16)
    value_rows = jnp.dot(packed, value_weight, preferred_element_type=jnp.float32).astype(
        jnp.bfloat16
    )
    query_head_rows = query_rows.reshape(token_count, KEY_VALUE_HEADS, group_size, HEAD_SIZE)
    query_seg = segment.astype(jnp.float32)
    seg_sent = segment.astype(jnp.bfloat16)
    start_state = (
        jnp.full((KEY_VALUE_HEADS, group_size, token_count), NEGATIVE_FILL, jnp.float32),
        jnp.zeros((KEY_VALUE_HEADS, group_size, token_count), jnp.float32),
        jnp.zeros((KEY_VALUE_HEADS, group_size, token_count, HEAD_SIZE), jnp.float32),
    )
    carry = start_state
    key_portion = lax.all_gather(key_rows, "ctx", axis=0, tiled=True)
    value_portion = lax.all_gather(value_rows, "ctx", axis=0, tiled=True)
    seg_piece = lax.all_gather(seg_sent, "ctx", axis=0, tiled=True)
    token_rows = key_portion.shape[0]
    block_step = 512
    event_count = token_rows // block_step
    key_block_list = key_portion.reshape(event_count, block_step, KEY_VALUE_HEADS, HEAD_SIZE)
    value_block_list = value_portion.reshape(event_count, block_step, KEY_VALUE_HEADS, HEAD_SIZE)
    seg_blocks = seg_piece.astype(jnp.float32).reshape(event_count, block_step)
    offsets = jnp.arange(event_count, dtype=jnp.int32) * block_step

    def one_block(state, inputs):
        key_tile_rows, value_block, seg_block, offset = inputs
        key_pos = offset + jnp.arange(block_step, dtype=jnp.int32)
        allowed = (seg_block[None, :] == query_seg[:, None]) & (
            key_pos[None, :] <= own_position[:, None]
        )
        best, total_tokens, accum = state
        logit_scores = (
            jnp.einsum(
                "qxli,oxi->xlqo", query_head_rows, key_tile_rows, preferred_element_type=jnp.float32
            )
            * score_scale
        )
        logit_scores = jnp.where(allowed, logit_scores, NEGATIVE_FILL)
        fresh = jnp.maximum(best, jnp.max(logit_scores, axis=-1))
        softmax_weights = jnp.where(allowed, jnp.exp(logit_scores - fresh[..., None]), 0.0)
        shrink = jnp.exp(best - fresh)
        total_tokens = total_tokens * shrink + jnp.sum(softmax_weights, axis=-1)
        accum = accum * shrink[..., None] + jnp.einsum(
            "qlwc,cqh->qlwh",
            softmax_weights.astype(jnp.bfloat16),
            value_block,
            preferred_element_type=jnp.float32,
        )
        state = (fresh, total_tokens, accum)
        return (state, None)

    carry, _ = lax.scan(one_block, carry, (key_block_list, value_block_list, seg_blocks, offsets))
    best, total_tokens, accum = carry
    result = (
        (accum / total_tokens[..., None])
        .transpose(2, 0, 1, 3)
        .reshape(token_count, QUERY_HEADS * HEAD_SIZE)
        .astype(jnp.bfloat16)
    )
    return result


def solution(mesh):
    return jax.shard_map(
        on_device,
        mesh=mesh,
        in_specs=(P(("dp", "ctx"), None), P(("dp", "ctx")), P(("dp", "ctx")), P(), P(), P()),
        out_specs=P(("dp", "ctx"), None),
        check_vma=False,
    )
```

profile of v0, /device:TPU:23, one launch (start us, length us, event | category | flops | bytes accessed | tf_op | source)
XLA Modules:
  0.0 209.7 jit_solution(15542477715000390240)
XLA Ops:
  8.9 2.4 %scatter_custom_fusion = s32[512]{0:T(512)S(1)} fusion(s32[512]{0:T(512)S(1)} %compare_select_fusion.1, s32[512]{0:T(512)S(1)} %get-tuple-element.167, s32[]{:T(128)} %constant.60.clone.1), kind=kCustom, calls=%fused_computation.56 | custom fusion | bytes 2052 | tf_op jit(solution)/shard_map/scatter | solution.py:43
  12.0 4.5 %all-to-all-start = ((s32[8,1,64]{2,1,0:T(1,128)}), s32[8,1,64]{2,1,0:T(1,128)S(1)}, u32[]{:S(2)}, u32[]{:S(2)}) async-start(s32[8,1,64]{2,1,0:T(1,128)} %all_to_all.9), calls=%async_computation | async-start | bytes 8192 | tf_op jit(solution)/shard_map/all_to_all | solution.py:48
  16.5 4.2 %scatter_custom_fusion.1 = bf16[512,1024]{1,0:T(8,128)(2,1)} fusion(s32[512]{0:T(512)S(1)} %compare_select_fusion.1, bf16[512,1024]{1,0:T(8,128)(2,1)} %param.8, bf16[]{:T(256)} %constant.59.clone.1), kind=kCustom, calls=%fused_computation.36 | custom fusion | bytes 1049088 | tf_op jit(solution)/shard_map/scatter | solution.py:37
  20.7 4.2 %all-to-all-start.1 = ((bf16[8,64,1024]{2,1,0:T(8,128)(2,1)}), bf16[8,64,1024]{2,1,0:T(8,128)(2,1)S(1)}, u32[]{:S(2)}, u32[]{:S(2)}) async-start(bf16[8,64,1024]{2,1,0:T(8,128)(2,1)} %bitcast.4), calls=%async_computation.1 | async-start | bytes 2097152 | tf_op jit(solution)/shard_map/all_to_all | solution.py:47
  26.3 11.3 %all-to-all-done.1 = bf16[8,64,1024]{2,1,0:T(8,128)(2,1)S(1)} async-done(((bf16[8,64,1024]{2,1,0:T(8,128)(2,1)}), bf16[8,64,1024]{2,1,0:T(8,128)(2,1)S(1)}, u32[]{:S(2)}, u32[]{:S(2)}) %all-to-all-start.1) | async-done | bytes 1048608 | tf_op jit(solution)/shard_map/all_to_all | solution.py:47
  38.6 3.5 %scatter_custom_fusion.2 = bf16[512,1024]{1,0:T(8,128)(2,1)S(1)} fusion(s32[512]{0:T(512)S(1)} %bitcast.76, bf16[512,1024]{1,0:T(8,128)(2,1)} %bitcast.72, bf16[]{:T(256)} %constant.59.clone.1), kind=kCustom, calls=%fused_computation.34 | custom fusion | bytes 1049088 | tf_op jit(solution)/shard_map/scatter | solution.py:53
  42.1 2.2 %convolution_convert_fusion.1 = bf16[512,256]{1,0:T(8,128)(2,1)} fusion(bf16[512,1024]{1,0:T(8,128)(2,1)S(1)} %scatter_custom_fusion.2, bf16[1024,256]{1,0:T(8,128)(2,1)} %param.13), kind=kOutput, calls=%fused_computation.31 | convolution fusion | flops 268566528 | bytes 1835008 | tf_op jit(solution)/shard_map/dot_general | solution.py:57
  44.4 2.2 %convolution_convert_fusion.2 = bf16[512,256]{1,0:T(8,128)(2,1)} fusion(bf16[512,1024]{1,0:T(8,128)(2,1)S(1)} %scatter_custom_fusion.2, bf16[1024,256]{1,0:T(8,128)(2,1)} %param.12), kind=kOutput, calls=%fused_computation.32 | convolution fusion | flops 268566528 | bytes 1835008 | tf_op jit(solution)/shard_map/dot_general | solution.py:56
  46.7 9.5 %all-gather = bf16[8,1,512]{2,1,0:T(2,128)(2,1)S(1)} all-gather(bf16[1,1,512]{2,1,0:T(2,128)(2,1)S(1)} %reshape.121), channel_id=1, replica_groups=mesh['dp'=4,'ctx'=8] {'ctx'}, dimensions={0}, use_global_device_ids=true | all-gather | bytes 9216 | tf_op jit(solution)/shard_map/all_gather | solution.py:71
  56.2 2.2 %convolution_convert_fusion = bf16[512,1024]{1,0:T(8,128)(2,1)} fusion(bf16[512,1024]{1,0:T(8,128)(2,1)S(1)} %scatter_custom_fusion.2, bf16[1024,1024]{1,0:T(8,128)(2,1)S(1)} %copy-done), kind=kOutput, calls=%fused_computation.30 | convolution fusion | flops 1074266112 | bytes 4194304 | tf_op jit(solution)/shard_map/dot_general | solution.py:55
  58.5 2.6 %reshape.91 = bf16[512,2,4,128]{3,2,1,0:T(4,128)(2,1)} reshape(bf16[512,1024]{1,0:T(8,128)(2,1)} %convolution_convert_fusion) | data formatting | bytes 2097152 | tf_op jit(solution)/shard_map/reshape | solution.py:60
  62.4 10.6 %all-gather.6.cloned.1.call-done = bf16[4096,256]{1,0:T(8,128)(2,1)} async-done(((bf16[512,256]{1,0:T(8,128)(2,1)}), bf16[4096,256]{1,0:T(8,128)(2,1)}) %all-gather.6.cloned.1.call-update) | async-done | bytes 2097168 | tf_op jit(solution)/shard_map/all_gather | solution.py:70
  73.0 4.0 %reshape.92 = bf16[8,512,2,128]{3,2,1,0:T(2,128)(2,1)} reshape(bf16[4096,256]{1,0:T(8,128)(2,1)} %all-gather.6.cloned.1.call-done) | data formatting | bytes 4194304 | tf_op jit(solution)/shard_map/reshape | solution.py:76
  76.9 25.8 %all-gather.4.cloned.1.call-done = bf16[4096,256]{1,0:T(8,128)(2,1)} async-done(((bf16[512,256]{1,0:T(8,128)(2,1)}), bf16[4096,256]{1,0:T(8,128)(2,1)}) %all-gather.4.cloned.1.call-update) | async-done | bytes 2097168 | tf_op jit(solution)/shard_map/all_gather | solution.py:69
  102.8 4.0 %reshape.90 = bf16[8,512,2,128]{3,2,1,0:T(2,128)(2,1)} reshape(bf16[4096,256]{1,0:T(8,128)(2,1)} %all-gather.4.cloned.1.call-done) | data formatting | bytes 4194304 | tf_op jit(solution)/shard_map/reshape | solution.py:75
  106.8 91.8 %while.15 = (s32[]{:T(128)}, f32[2,4,512]{2,1,0:T(4,128)S(1)}, f32[2,4,512]{2,1,0:T(4,128)S(1)}, f32[2,4,512,128]{3,2,1,0:T(8,128)}, f32[8,512]{1,0:T(8,128)S(1)...) while((s32[]{:T(128)}, f32[2,4,512]{2,1,0:T(4,128)S(1)}, ...), condition=%wide.region_9.10_spmd.clone, body=%wide.region_6.9_spmd.clone.sunk | while | flops 1103385600 | bytes 50086116 | solution.py:107
  108.3 1.4 constant_dynamic-slice_fusion.6
  109.7 1.6 fusion.43
  111.3 2.0 fusion.44
  113.4 3.5 %fusion.46 = f32[2,4,512,128]{3,2,1,0:T(8,128)S(1)} fusion(f32[2,4,512,128]{3,2,1,0:T(8,128)S(1)} %copy-done.1, f32[2,512,512,4]{2,1,3,0:T(8,128)S(1)} %get-tuple-element.250, f32[2,4,512]{2,1,0:T(4,128)S(1)} %select_maximum_fusion.2, pred[512,512]{0,1:T(8,128)(4,1)S(1)} %compare_and_fusion.2, f32[2,4,512]{2,1,0:T(4,128)S(1)} %get-tuple-element.252, ...), kind=kOutput, calls=%fused_computation.12.clone.1 | convolution fusion | flops 548929536 | bytes 13139969 | tf_op jit(solution)/shard_map/while/body/eval_jaxpr/qlwc,cqh->qlwh/dot_general | solution.py:98
  119.7 1.4 constant_dynamic-slice_fusion.6
  121.1 1.6 fusion.43
  122.8 2.0 fusion.44
  124.9 3.5 %fusion.46 = f32[2,4,512,128]{3,2,1,0:T(8,128)S(1)} fusion(f32[2,4,512,128]{3,2,1,0:T(8,128)S(1)} %copy-done.1, f32[2,512,512,4]{2,1,3,0:T(8,128)S(1)} %get-tuple-element.250, f32[2,4,512]{2,1,0:T(4,128)S(1)} %select_maximum_fusion.2, pred[512,512]{0,1:T(8,128)(4,1)S(1)} %compare_and_fusion.2, f32[2,4,512]{2,1,0:T(4,128)S(1)} %get-tuple-element.252, ...), kind=kOutput, calls=%fused_computation.12.clone.1 | convolution fusion | flops 548929536 | bytes 13139969 | tf_op jit(solution)/shard_map/while/body/eval_jaxpr/qlwc,cqh->qlwh/dot_general | solution.py:98
  131.2 1.4 constant_dynamic-slice_fusion.6
  132.6 1.6 fusion.43
  134.2 2.0 fusion.44
  136.3 3.5 %fusion.46 = f32[2,4,512,128]{3,2,1,0:T(8,128)S(1)} fusion(f32[2,4,512,128]{3,2,1,0:T(8,128)S(1)} %copy-done.1, f32[2,512,512,4]{2,1,3,0:T(8,128)S(1)} %get-tuple-element.250, f32[2,4,512]{2,1,0:T(4,128)S(1)} %select_maximum_fusion.2, pred[512,512]{0,1:T(8,128)(4,1)S(1)} %compare_and_fusion.2, f32[2,4,512]{2,1,0:T(4,128)S(1)} %get-tuple-element.252, ...), kind=kOutput, calls=%fused_computation.12.clone.1 | convolution fusion | flops 548929536 | bytes 13139969 | tf_op jit(solution)/shard_map/while/body/eval_jaxpr/qlwc,cqh->qlwh/dot_general | solution.py:98
  142.7 1.4 constant_dynamic-slice_fusion.6
  144.1 1.6 fusion.43
  145.7 2.0 fusion.44
  147.8 3.5 %fusion.46 = f32[2,4,512,128]{3,2,1,0:T(8,128)S(1)} fusion(f32[2,4,512,128]{3,2,1,0:T(8,128)S(1)} %copy-done.1, f32[2,512,512,4]{2,1,3,0:T(8,128)S(1)} %get-tuple-element.250, f32[2,4,512]{2,1,0:T(4,128)S(1)} %select_maximum_fusion.2, pred[512,512]{0,1:T(8,128)(4,1)S(1)} %compare_and_fusion.2, f32[2,4,512]{2,1,0:T(4,128)S(1)} %get-tuple-element.252, ...), kind=kOutput, calls=%fused_computation.12.clone.1 | convolution fusion | flops 548929536 | bytes 13139969 | tf_op jit(solution)/shard_map/while/body/eval_jaxpr/qlwc,cqh->qlwh/dot_general | solution.py:98
  154.2 1.4 constant_dynamic-slice_fusion.6
  155.6 1.6 fusion.43
  157.2 2.0 fusion.44
  159.3 3.5 %fusion.46 = f32[2,4,512,128]{3,2,1,0:T(8,128)S(1)} fusion(f32[2,4,512,128]{3,2,1,0:T(8,128)S(1)} %copy-done.1, f32[2,512,512,4]{2,1,3,0:T(8,128)S(1)} %get-tuple-element.250, f32[2,4,512]{2,1,0:T(4,128)S(1)} %select_maximum_fusion.2, pred[512,512]{0,1:T(8,128)(4,1)S(1)} %compare_and_fusion.2, f32[2,4,512]{2,1,0:T(4,128)S(1)} %get-tuple-element.252, ...), kind=kOutput, calls=%fused_computation.12.clone.1 | convolution fusion | flops 548929536 | bytes 13139969 | tf_op jit(solution)/shard_map/while/body/eval_jaxpr/qlwc,cqh->qlwh/dot_general | solution.py:98
  165.7 1.4 constant_dynamic-slice_fusion.6
  167.1 1.6 fusion.43
  168.7 2.0 fusion.44
  170.8 3.5 %fusion.46 = f32[2,4,512,128]{3,2,1,0:T(8,128)S(1)} fusion(f32[2,4,512,128]{3,2,1,0:T(8,128)S(1)} %copy-done.1, f32[2,512,512,4]{2,1,3,0:T(8,128)S(1)} %get-tuple-element.250, f32[2,4,512]{2,1,0:T(4,128)S(1)} %select_maximum_fusion.2, pred[512,512]{0,1:T(8,128)(4,1)S(1)} %compare_and_fusion.2, f32[2,4,512]{2,1,0:T(4,128)S(1)} %get-tuple-element.252, ...), kind=kOutput, calls=%fused_computation.12.clone.1 | convolution fusion | flops 548929536 | bytes 13139969 | tf_op jit(solution)/shard_map/while/body/eval_jaxpr/qlwc,cqh->qlwh/dot_general | solution.py:98
  178.5 1.6 fusion.43
  180.1 2.0 fusion.44
  182.2 3.5 %fusion.46 = f32[2,4,512,128]{3,2,1,0:T(8,128)S(1)} fusion(f32[2,4,512,128]{3,2,1,0:T(8,128)S(1)} %copy-done.1, f32[2,512,512,4]{2,1,3,0:T(8,128)S(1)} %get-tuple-element.250, f32[2,4,512]{2,1,0:T(4,128)S(1)} %select_maximum_fusion.2, pred[512,512]{0,1:T(8,128)(4,1)S(1)} %compare_and_fusion.2, f32[2,4,512]{2,1,0:T(4,128)S(1)} %get-tuple-element.252, ...), kind=kOutput, calls=%fused_computation.12.clone.1 | convolution fusion | flops 548929536 | bytes 13139969 | tf_op jit(solution)/shard_map/while/body/eval_jaxpr/qlwc,cqh->qlwh/dot_general | solution.py:98
  190.0 1.6 fusion.43
  191.6 2.0 fusion.44
  193.7 3.5 %fusion.46 = f32[2,4,512,128]{3,2,1,0:T(8,128)S(1)} fusion(f32[2,4,512,128]{3,2,1,0:T(8,128)S(1)} %copy-done.1, f32[2,512,512,4]{2,1,3,0:T(8,128)S(1)} %get-tuple-element.250, f32[2,4,512]{2,1,0:T(4,128)S(1)} %select_maximum_fusion.2, pred[512,512]{0,1:T(8,128)(4,1)S(1)} %compare_and_fusion.2, f32[2,4,512]{2,1,0:T(4,128)S(1)} %get-tuple-element.252, ...), kind=kOutput, calls=%fused_computation.12.clone.1 | convolution fusion | flops 548929536 | bytes 13139969 | tf_op jit(solution)/shard_map/while/body/eval_jaxpr/qlwc,cqh->qlwh/dot_general | solution.py:98
  198.6 1.9 fusion.16
  201.3 1.5 convert_element_type.44
  (123 shorter events, 33.4 us)
Async XLA Ops:
  6.5 49.7 %copy-start = (bf16[1024,1024]{1,0:T(8,128)(2,1)S(1)}, bf16[1024,1024]{1,0:T(8,128)(2,1)}, u32[]{:S(2)}) copy-start(bf16[1024,1024]{1,0:T(8,128)(2,1)} %param.11) | copy-start | bytes 6291460
  12.0 8.7 %all-to-all-start = ((s32[8,1,64]{2,1,0:T(1,128)}), s32[8,1,64]{2,1,0:T(1,128)S(1)}, u32[]{:S(2)}, u32[]{:S(2)}) async-start(s32[8,1,64]{2,1,0:T(1,128)} %all_to_all.9), calls=%async_computation | async-start | bytes 8192 | tf_op jit(solution)/shard_map/all_to_all | solution.py:48
  16.5 30.1 %copy-start.4 = (s32[512]{0:T(512)S(1)}, s32[512]{0:T(512)}, u32[]{:S(2)}) copy-start(s32[512]{0:T(512)} %param.10) | copy-start | bytes 6148
  20.7 16.9 %all-to-all-start.1 = ((bf16[8,64,1024]{2,1,0:T(8,128)(2,1)}), bf16[8,64,1024]{2,1,0:T(8,128)(2,1)S(1)}, u32[]{:S(2)}, u32[]{:S(2)}) async-start(bf16[8,64,1024]{2,1,0:T(8,128)(2,1)} %bitcast.4), calls=%async_computation.1 | async-start | bytes 2097152 | tf_op jit(solution)/shard_map/all_to_all | solution.py:47
  24.9 48.0 %all-gather.6.cloned.1.call-start = ((), (), s32[]{:S(2)}) async-start(), calls=%async_computation.3 | async-start | bytes 2359296 | tf_op jit(solution)/shard_map/all_gather | solution.py:70
  37.7 1.0 copy-start.3
  44.3 58.5 %all-gather.4.cloned.1.call-start = ((), (), s32[]{:S(2)}) async-start(), calls=%async_computation.2 | async-start | bytes 2359296 | tf_op jit(solution)/shard_map/all_gather | solution.py:69
  111.3 2.1 copy-start.1
  116.9 1.3 copy-start.2
  122.8 2.1 copy-start.1
  128.4 1.3 copy-start.2
  134.2 2.1 copy-start.1
  139.8 1.3 copy-start.2
  145.7 2.1 copy-start.1
  151.3 1.3 copy-start.2
  157.2 2.1 copy-start.1
  162.8 1.3 copy-start.2
  168.7 2.1 copy-start.1
  174.3 1.3 copy-start.2
  180.1 2.1 copy-start.1
  185.8 1.3 copy-start.2
  191.6 2.1 copy-start.1
  197.2 1.3 copy-start.2
Sparse Core Ops, SparseCore 0:
  44.4 28.4 all-gather.5
  74.8 27.8 all-gather.3
where the time goes:
time: 213 us; the launch traced here: 210 us
  local copies, waits for them, and re-layouts  53.3 us (25%)
  waiting for transfers between devices  47.8 us (22%)
  matrix products  47.3 us (22%)
  other arithmetic  28.9 us (14%)
  between operations  13.5 us (6%)
  blocking collectives  9.54 us (4%)
  starting transfers between devices  8.76 us (4%)
    dot_general x8, matrix products, one_block(): jnp.einsum('qlwc,cqh->qlwh', softmax_weights.astype(jnp.bfloat16), value_...  28.1 us
    all_gather x1, waiting for transfers between devices, on_device(): key_portion = lax.all_gather(key_rows, 'ctx', axis=0, tiled=True)  25.8 us
    reduce_sum x8, other arithmetic, one_block(): total_tokens = total_tokens * shrink + jnp.sum(softmax_weights, axis=-1)  16.4 us
    dynamic_slice x24, local copies, waits for them, and re-layouts, on_device(): lax.scan(one_block, carry, (key_block_list, value_block_list, seg_blocks,...  15.9 us
    dot_general x8, matrix products, one_block(): jnp.einsum('qxli,oxi->xlqo', query_head_rows, key_tile_rows, preferred_el...  12.6 us
    all_to_all x1, waiting for transfers between devices, on_device(): lax.all_to_all(send_rows, 'ctx', split_axis=0, concat_axis=0, tiled=True)  11.3 us
    all_gather x1, waiting for transfers between devices, on_device(): value_portion = lax.all_gather(value_rows, 'ctx', axis=0, tiled=True)  10.6 us
    while x40, local copies, waits for them, and re-layouts  10.6 us
  transfers between devices with their start and end apart: 4, of which 3 were waited for; matrix products, arithmetic and copies ran while one was open for 9% of the time, Pallas kernels for 0%

commit v1 on v0

--- a/solution.py
+++ b/solution.py
@@ -1,20 +1,309 @@
+import functools
 import math
 
 import jax
 import jax.numpy as jnp
 from jax import lax
+from jax.experimental import pallas as pl
+from jax.experimental.pallas import tpu as pltpu
 from jax.sharding import PartitionSpec as P
 
 QUERY_HEADS = 8
 KEY_VALUE_HEADS = 2
 HEAD_SIZE = 128
+GROUP = QUERY_HEADS // KEY_VALUE_HEADS
 BLOCKS = 8
-
+SEGMENTS = 4
+LANES = 128
 
 NEGATIVE_FILL = -1e30
-
-
-def on_device(events, destination, segment, w_query, key_weight, value_weight):
+SCALE = math.log2(math.e) / math.sqrt(HEAD_SIZE)
+NT = (((1,), (1,)), ((), ()))
+
+
+def fused_kernel(
+    dest_ref, seg_ref, events_hbm, wq_hbm, wk_hbm, wv_hbm, out_ref,
+    events, wq, wk, wv, rows_sorted, info_send, info, kv_send, kv, q_local, q_all,
+    pair_pos, pair_start, key_pos, values_t, best, accum, o_send, o_recv,
+    load_sem, info_ssem, info_rsem, kv_ssem, kv_rsem, q_sem, o_ssem, o_rsem,
+):
+    tokens = events.shape[0]
+    n = BLOCKS
+    blk = tokens // n
+    wide = GROUP * HEAD_SIZE
+    me = lax.axis_index("ctx")
+    core = me % 2
+    chip = me // 2
+    sibling = chip * 2 + 1 - core
+    f32 = jnp.float32
+
+    loads = [
+        pltpu.make_async_copy(src, dst, load_sem.at[k])
+        for k, (src, dst) in enumerate(
+            ((events_hbm, events), (wk_hbm, wk), (wv_hbm, wv), (wq_hbm, wq))
+        )
+    ]
+    for load in loads:
+        load.start()
+
+    barrier = pltpu.get_barrier_semaphore()
+    for d in range(1, n):
+        pl.semaphore_signal(
+            barrier, inc=1, device_id={"ctx": (me + d) % n}, device_id_type=pl.DeviceIdType.MESH
+        )
+
+    dest = dest_ref[...]
+    target = jnp.zeros_like(dest)
+    for j in range(1, n):
+        target = target + (dest >= j * tokens).astype(jnp.int32)
+    row_of = lax.broadcasted_iota(jnp.int32, (n, tokens), 0)
+    base = jnp.min(
+        jnp.where(jnp.broadcast_to(target, (n, tokens)) == row_of, dest.astype(f32), 1e9),
+        axis=1, keepdims=True,
+    )
+    below = jnp.sum(
+        jnp.where(jnp.broadcast_to(seg_ref[...], (n, tokens)) < row_of, 1.0, 0.0),
+        axis=1, keepdims=True,
+    )
+    info_send[0:n, :] = jnp.broadcast_to(base, (n, LANES))
+    info_send[n : 2 * n, :] = jnp.broadcast_to(below, (n, LANES))
+    info[me] = info_send[...]
+
+    lane = lax.broadcasted_iota(jnp.int32, (1, tokens), 1)
+    rank = target * blk + lane % blk
+    place = lax.broadcasted_iota(jnp.int32, (tokens, tokens), 0) == rank
+    order = jnp.where(place, 1.0, 0.0).astype(jnp.bfloat16)
+
+    pl.semaphore_wait(barrier, n - 1)
+
+    def info_copy(d):
+        peer = (me + d) % n
+        return pltpu.make_async_remote_copy(
+            info_send, info.at[me], info_ssem.at[d], info_rsem.at[me],
+            device_id={"ctx": peer}, device_id_type=pl.DeviceIdType.MESH,
+        )
+
+    for d in range(1, n):
+        info_copy(d).start()
+
+    loads[0].wait()
+    rows_sorted[...] = jnp.dot(order, events[...], preferred_element_type=f32).astype(jnp.bfloat16)
+    loads[1].wait()
+    loads[2].wait()
+    keys = jnp.dot(rows_sorted[...], wk[...], preferred_element_type=f32).astype(jnp.bfloat16)
+    values = jnp.dot(rows_sorted[...], wv[...], preferred_element_type=f32).astype(jnp.bfloat16)
+    for h in range(KEY_VALUE_HEADS):
+        cols = slice(h * HEAD_SIZE, (h + 1) * HEAD_SIZE)
+        kv_send[h, :, :, 0:HEAD_SIZE] = keys[:, cols].reshape(n, blk, HEAD_SIZE)
+        kv_send[h, :, :, HEAD_SIZE:] = values[:, cols].reshape(n, blk, HEAD_SIZE)
+
+    def kv_copy(j, d, c):
+        to_chip = (chip + d) % (n // 2)
+        return pltpu.make_async_remote_copy(
+            kv_send.at[c, j], kv.at[j, me], kv_ssem.at[j, 2 * d + c], kv_rsem.at[j, me],
+            device_id={"ctx": to_chip * 2 + c}, device_id_type=pl.DeviceIdType.MESH,
+        )
+
+    def sibling_kv(j):
+        return pltpu.make_async_remote_copy(
+            kv_send.at[1 - core, j], kv.at[j, me], kv_ssem.at[j, 0], kv_rsem.at[j, me],
+            device_id={"ctx": sibling}, device_id_type=pl.DeviceIdType.MESH,
+        )
+
+    @pl.loop(0, n)
+    def _(j):
+        for d in range(1, n // 2):
+            for c in range(2):
+                kv_copy(j, d, c).start()
+        sibling_kv(j).start()
+        kv[j, me] = kv_send[core, j]
+
+    loads[3].wait()
+    for h in range(KEY_VALUE_HEADS):
+        query = jnp.dot(
+            rows_sorted[...], wq[:, h * wide : (h + 1) * wide], preferred_element_type=f32
+        ).astype(jnp.bfloat16)
+        for e in range(GROUP):
+            q_local[h, :, e] = query[:, e * HEAD_SIZE : (e + 1) * HEAD_SIZE].reshape(
+                n, blk, HEAD_SIZE
+            )
+    q_copy = pltpu.make_async_remote_copy(
+        q_local.at[1 - core], q_all.at[core], q_sem.at[0], q_sem.at[1],
+        device_id={"ctx": sibling}, device_id_type=pl.DeviceIdType.MESH,
+    )
+    q_copy.start()
+    q_all[core] = q_local[core]
+
+    best[...] = jnp.full(best.shape, NEGATIVE_FILL, f32)
+    accum[...] = jnp.zeros(accum.shape, f32)
+    values_t[HEAD_SIZE:, :] = jnp.ones((values_t.shape[0] - HEAD_SIZE, tokens), jnp.bfloat16)
+
+    for d in range(1, n):
+        source = (me + d) % n
+        pltpu.make_async_remote_copy(
+            info_send, info.at[source], info_ssem.at[d], info_rsem.at[source],
+            device_id={"ctx": source}, device_id_type=pl.DeviceIdType.MESH,
+        ).wait_recv()
+
+    counts = jnp.sum(info[:, n : 2 * n, :], axis=0)
+    pair = lax.broadcasted_iota(jnp.int32, (n, 2 * blk), 1)
+    for c in range(n // 2):
+        where = jnp.where(pair < blk, info[2 * c, 0:n, :], info[2 * c + 1, 0:n, :])
+        pair_pos[c] = where + (pair % blk).astype(f32)
+    mine = pair_pos[chip]
+    start = jnp.zeros_like(mine)
+    for s in range(1, SEGMENTS):
+        edge = jnp.broadcast_to(counts[s : s + 1, :], mine.shape)
+        start = jnp.maximum(start, jnp.where(mine >= edge, edge, 0.0))
+    pair_start[...] = start
+
+    q_copy.wait_recv()
+
+    def o_copy(i):
+        return pltpu.make_async_remote_copy(
+            o_send.at[i], o_recv.at[core, chip], o_ssem.at[i], o_rsem.at[me],
+            device_id={"ctx": i}, device_id_type=pl.DeviceIdType.MESH,
+        )
+
+    @pl.loop(0, n)
+    def _(j):
+        for d in range(1, n):
+            source = (me + d) % n
+            pltpu.make_async_remote_copy(
+                kv_send.at[0, j], kv.at[j, source], kv_ssem.at[j, 0], kv_rsem.at[j, source],
+                device_id={"ctx": source}, device_id_type=pl.DeviceIdType.MESH,
+            ).wait_recv()
+        block = kv[j].reshape(tokens, 2 * HEAD_SIZE)
+        values_t[0:HEAD_SIZE, :] = block[:, HEAD_SIZE:].astype(f32).T.astype(jnp.bfloat16)
+        for s in range(n):
+            key_pos[s * blk : (s + 1) * blk, :] = info[s, pl.ds(j, 1), :] + lax.broadcasted_iota(
+                jnp.int32, (blk, LANES), 0
+            ).astype(f32)
+        key_tile = block[:, 0:HEAD_SIZE]
+
+        @pl.loop(j, n)
+        def _(i):
+            here = pair_pos[chip, pl.ds(i, 1), :]
+            start = pair_start[pl.ds(i, 1), :]
+            at = key_pos[...]
+            bias = jnp.where((at >= start) & (at <= here), 0.0, NEGATIVE_FILL)
+            bias = jnp.concatenate([bias, bias], axis=1)
+            for half in range(2):
+                cols = slice(half * 4 * blk, (half + 1) * 4 * blk)
+                query = jnp.concatenate(
+                    [
+                        q_all[c, i, 2 * half + e]
+                        for e in range(2)
+                        for c in range(2)
+                    ],
+                    axis=0,
+                )
+                scores = lax.dot_general(key_tile, query, NT, preferred_element_type=f32) + bias
+                old = best[i, :, cols]
+                fresh = jnp.maximum(old, jnp.max(scores, axis=0, keepdims=True))
+                weights = jnp.exp2((scores - fresh) * SCALE).astype(jnp.bfloat16)
+                best[i, :, cols] = fresh
+                accum[i, :, cols] = accum[i, :, cols] * jnp.exp2((old - fresh) * SCALE) + jnp.dot(
+                    values_t[...], weights, preferred_element_type=f32
+                )
+
+            @pl.when(i == j)
+            def _():
+                for e in range(GROUP):
+                    cols = slice(e * 2 * blk, (e + 1) * 2 * blk)
+                    mixed = accum[i, 0:HEAD_SIZE, cols] / accum[i, HEAD_SIZE : HEAD_SIZE + 1, cols]
+                    o_send[i, :, e * HEAD_SIZE : (e + 1) * HEAD_SIZE] = mixed.T.astype(jnp.bfloat16)
+
+                @pl.when(i != me)
+                def _():
+                    o_copy(i).start()
+
+                @pl.when(i == me)
+                def _():
+                    o_recv[core, chip] = o_send[i]
+
+    origin = (me * tokens).astype(f32)
+    into = jnp.concatenate([pair_pos[c, pl.ds(me, 1), :] for c in range(n // 2)], axis=1) - origin
+    row = lax.broadcasted_iota(jnp.int32, (tokens, tokens), 0).astype(f32)
+    order = jnp.where(row == into, 1.0, 0.0).astype(jnp.bfloat16)
+    for d in range(1, n):
+        source = (me + d) % n
+        pltpu.make_async_remote_copy(
+            o_send.at[0], o_recv.at[source % 2, source // 2], o_ssem.at[0], o_rsem.at[source],
+            device_id={"ctx": source}, device_id_type=pl.DeviceIdType.MESH,
+        ).wait_recv()
+    for c in range(2):
+        got = o_recv[c].reshape(tokens, wide)
+        out_ref[:, c * wide : (c + 1) * wide] = jnp.dot(
+            order, got, preferred_element_type=f32
+        ).astype(jnp.bfloat16)
+
+    for d in range(1, n):
+        info_copy(d).wait_send()
+    q_copy.wait_send()
+
+    @pl.loop(0, n)
+    def _(j):
+        for d in range(1, n // 2):
+            for c in range(2):
+                kv_copy(j, d, c).wait_send()
+        sibling_kv(j).wait_send()
+
+        @pl.when(j != me)
+        def _():
+            o_copy(j).wait_send()
+
+
+def on_device_fused(events, destination, segment, w_query, key_weight, value_weight):
+    tokens, width = events.shape
+    n = BLOCKS
+    blk = tokens // n
+    wide = GROUP * HEAD_SIZE
+    bf16, f32 = jnp.bfloat16, jnp.float32
+    vmem = pl.BlockSpec(memory_space=pltpu.VMEM)
+    hbm = pl.BlockSpec(memory_space=pl.ANY)
+    dma = pltpu.SemaphoreType.DMA
+    return pl.pallas_call(
+        fused_kernel,
+        out_shape=jax.ShapeDtypeStruct((tokens, QUERY_HEADS * HEAD_SIZE), bf16),
+        in_specs=[vmem, vmem, hbm, hbm, hbm, hbm],
+        out_specs=vmem,
+        scratch_shapes=[
+            pltpu.VMEM((tokens, width), bf16),
+            pltpu.VMEM(w_query.shape, bf16),
+            pltpu.VMEM(key_weight.shape, bf16),
+            pltpu.VMEM(value_weight.shape, bf16),
+            pltpu.VMEM((tokens, width), bf16),
+            pltpu.VMEM((2 * n, LANES), f32),
+            pltpu.VMEM((n, 2 * n, LANES), f32),
+            pltpu.VMEM((KEY_VALUE_HEADS, n, blk, 2 * HEAD_SIZE), bf16),
+            pltpu.VMEM((n, n, blk, 2 * HEAD_SIZE), bf16),
+            pltpu.VMEM((KEY_VALUE_HEADS, n, GROUP, blk, HEAD_SIZE), bf16),
+            pltpu.VMEM((2, n, GROUP, blk, HEAD_SIZE), bf16),
+            pltpu.VMEM((n // 2, n, LANES), f32),
+            pltpu.VMEM((n, LANES), f32),
+            pltpu.VMEM((tokens, LANES), f32),
+            pltpu.VMEM((HEAD_SIZE + 16, tokens), bf16),
+            pltpu.VMEM((n, 1, GROUP * 2 * blk), f32),
+            pltpu.VMEM((n, HEAD_SIZE + 16, GROUP * 2 * blk), f32),
+            pltpu.VMEM((n, 2 * blk, wide), bf16),
+            pltpu.VMEM((2, n // 2, 2 * blk, wide), bf16),
+            dma((4,)),
+            dma((n,)),
+            dma((n,)),
+            dma((n, n)),
+            dma((n, n)),
+            dma((2,)),
+            dma((n,)),
+            dma((n,)),
+        ],
+        compiler_params=pltpu.CompilerParams(
+            collective_id=0, has_side_effects=True, vmem_limit_bytes=56 * 1024 * 1024
+        ),
+    )(destination.reshape(1, tokens), segment.reshape(1, tokens), events, w_query, key_weight, value_weight)
+
+
+def on_device_general(events, destination, segment, w_query, key_weight, value_weight):
     token_count = events.shape[0]
     width = events.shape[1]
     ndevices = lax.axis_size("ctx")
@@ -28,7 +317,8 @@
     bucket = token_count // BLOCKS
     own_position = myself * token_count + local_rows
     onehot = (target[:, None] == lanes[None, :]).astype(jnp.int32)
-    before = jnp.cumsum(onehot, axis=0) - onehot
+    earlier = (local_rows[None, :] < local_rows[:, None]).astype(jnp.float32)
+    before = jnp.dot(earlier, onehot.astype(jnp.float32)).astype(jnp.int32)
     slot = jnp.sum(before * onehot, axis=1)
     index = target * bucket + slot
     send_rows = (
@@ -116,6 +406,10 @@
 
 
 def solution(mesh):
+    def on_device(events, *rest):
+        fits = mesh.shape["ctx"] == BLOCKS and events.shape[0] == BLOCKS * LANES // 2
+        return (on_device_fused if fits else on_device_general)(events, *rest)
+
     return jax.shard_map(
         on_device,
         mesh=mesh,

time: 213 us -> 61.1 us (0.29); the launches traced: 210 us -> 60.9 us
  Pallas kernels: 0 us -> 58.7 us
  local copies, waits for them, and re-layouts: 53.3 us -> 2.26 us
  waiting for transfers between devices: 47.8 us -> 0 us
  matrix products: 47.3 us -> 0 us
  other arithmetic: 28.9 us -> 0 us
  between operations: 13.5 us -> 0.01 us
  blocking collectives: 9.54 us -> 0 us
  starting transfers between devices: 8.76 us -> 0 us
    pallas_call x0 -> x1, Pallas kernels: none -> 58.7 us  [on_device_fused(): pl.pallas_call(fused_kernel, out_shape=jax.ShapeDtypeStruct((tokens, QUER...]
    dot_general x19 -> x0, matrix products: 47.3 us -> none  [the longest x8 28.1 us: one_block(): jnp.einsum('qlwc,cqh->qlwh', softmax_weights.astype(jnp.bfloat16), value_...]
    all_gather x2 -> x0, waiting for transfers between devices: 36.4 us -> none  [the longest x1 25.8 us: on_device(): key_portion = lax.all_gather(key_rows, 'ctx', axis=0, tiled=True)]
    reduce_sum x9 -> x0, other arithmetic: 16.5 us -> none  [the longest x8 16.4 us: one_block(): total_tokens = total_tokens * shrink + jnp.sum(softmax_weights, axis=-1)]
    dynamic_slice x24 -> x0, local copies, waits for them, and re-layouts: 15.9 us -> none  [on_device(): lax.scan(one_block, carry, (key_block_list, value_block_list, seg_blocks,...]
    all_to_all x2 -> x0, waiting for transfers between devices: 11.3 us -> none  [the longest x1 11.3 us: on_device(): lax.all_to_all(send_rows, 'ctx', split_axis=0, concat_axis=0, tiled=True)]
    reshape x4 -> x0, local copies, waits for them, and re-layouts: 10.6 us -> none  [the longest x1 3.98 us: on_device(): key_portion.reshape(event_count, block_step, KEY_VALUE_HEADS, HEAD_SIZE)]
    while x40 -> x0, local copies, waits for them, and re-layouts: 10.6 us -> none
  transfers between devices with their start and end apart: 4 -> 0, of which waited for: 3 -> 0; matrix products, arithmetic and copies ran while one was open for 9% -> 0% of each run, Pallas kernels for 0% -> 0%
where the time goes in v1:
time: 61.1 us; the launch traced here: 60.9 us
  Pallas kernels  58.7 us (96%)
  local copies, waits for them, and re-layouts  2.26 us (4%)
    pallas_call x1, Pallas kernels, on_device_fused(): pl.pallas_call(fused_kernel, out_shape=jax.ShapeDtypeStruct((tokens, QUER...  58.7 us
    unnamed x1, local copies, waits for them, and re-layouts  2.26 us

profile of v1, /device:TPU:23, one launch (start us, length us, event | category | flops | bytes accessed | tf_op | source)
XLA Modules:
  0.0 60.9 jit_solution(3867493227004416094)
XLA Ops:
  0.0 58.7 %shard_map.64 = bf16[512,1024]{1,0:T(8,128)(2,1)} custom-call(s32[1,512]{1,0:T(1,128)} %bitcast.2, s32[1,512]{1,0:T(1,128)} %bitcast.3, bf16[512,1024]{1,0:T(8,128)(2,1)} %events_hbm.1, bf16[1024,1024]{1,0:T(8,128)(2,1)} %wq_hbm.1, bf16[1024,256]{1,0:T(8,128)(2,1)} %wk_hbm.1, bf16[1024,256]{1,0:T(8,128)(2,1)} %wv_hbm.1), custom_call_target="tpu_custom_call" | custom-call | tf_op jit(solution)/shard_map/pallas_call | solution.py:266
  58.7 2.3 %copy.8 = bf16[512,1024]{1,0:T(8,128)(2,1)} copy(bf16[512,1024]{1,0:T(8,128)(2,1)} %shard_map.64) | data formatting | bytes 2097152

commit v2 on v1

--- a/solution.py
+++ b/solution.py
@@ -23,7 +23,7 @@
 
 def fused_kernel(
     dest_ref, seg_ref, events_hbm, wq_hbm, wk_hbm, wv_hbm, out_ref,
-    events, wq, wk, wv, rows_sorted, info_send, info, kv_send, kv, q_local, q_all,
+    events, wq, wk, wv, rows_sorted, info_send, info, kv_send, kv, q_local, q_all, q_pairs,
     pair_pos, pair_start, key_pos, values_t, best, accum, o_send, o_recv,
     load_sem, info_ssem, info_rsem, kv_ssem, kv_rsem, q_sem, o_ssem, o_rsem,
 ):
@@ -158,6 +158,10 @@
     pair_start[...] = start
 
     q_copy.wait_recv()
+    for e in range(GROUP):
+        for c in range(2):
+            first = (2 * e + c) * blk
+            q_pairs[:, first : first + blk, :] = q_all[c, :, e]
 
     def o_copy(i):
         return pltpu.make_async_remote_copy(
@@ -188,24 +192,23 @@
             at = key_pos[...]
             bias = jnp.where((at >= start) & (at <= here), 0.0, NEGATIVE_FILL)
             bias = jnp.concatenate([bias, bias], axis=1)
-            for half in range(2):
-                cols = slice(half * 4 * blk, (half + 1) * 4 * blk)
-                query = jnp.concatenate(
-                    [
-                        q_all[c, i, 2 * half + e]
-                        for e in range(2)
-                        for c in range(2)
-                    ],
-                    axis=0,
+            halves = range(2)
+            wide_cols = [slice(h * 4 * blk, (h + 1) * 4 * blk) for h in halves]
+            old = [best[i, :, cols] for cols in wide_cols]
+            held = [accum[i, :, cols] for cols in wide_cols]
+            scores = [
+                lax.dot_general(
+                    key_tile, q_pairs[i, h * 4 * blk : (h + 1) * 4 * blk, :], NT, preferred_element_type=f32
                 )
-                scores = lax.dot_general(key_tile, query, NT, preferred_element_type=f32) + bias
-                old = best[i, :, cols]
-                fresh = jnp.maximum(old, jnp.max(scores, axis=0, keepdims=True))
-                weights = jnp.exp2((scores - fresh) * SCALE).astype(jnp.bfloat16)
-                best[i, :, cols] = fresh
-                accum[i, :, cols] = accum[i, :, cols] * jnp.exp2((old - fresh) * SCALE) + jnp.dot(
-                    values_t[...], weights, preferred_element_type=f32
-                )
+                + bias
+                for h in halves
+            ]
+            fresh = [jnp.maximum(old[h], jnp.max(scores[h], axis=0, keepdims=True)) for h in halves]
+            weights = [jnp.exp2((scores[h] - fresh[h]) * SCALE).astype(jnp.bfloat16) for h in halves]
+            added = [jnp.dot(values_t[...], weights[h], preferred_element_type=f32) for h in halves]
+            for h in halves:
+                best[i, :, wide_cols[h]] = fresh[h]
+                accum[i, :, wide_cols[h]] = held[h] * jnp.exp2((old[h] - fresh[h]) * SCALE) + added[h]
 
             @pl.when(i == j)
             def _():
@@ -280,6 +283,7 @@
             pltpu.VMEM((n, n, blk, 2 * HEAD_SIZE), bf16),
             pltpu.VMEM((KEY_VALUE_HEADS, n, GROUP, blk, HEAD_SIZE), bf16),
             pltpu.VMEM((2, n, GROUP, blk, HEAD_SIZE), bf16),
+            pltpu.VMEM((n, GROUP * 2 * blk, HEAD_SIZE), bf16),
             pltpu.VMEM((n // 2, n, LANES), f32),
             pltpu.VMEM((n, LANES), f32),
             pltpu.VMEM((tokens, LANES), f32),

time: 61.1 us -> 51 us (0.83)
  Pallas kernels: 58.7 us -> 48.6 us
    pallas_call x1, Pallas kernels: 58.7 us -> 48.6 us  [on_device_fused(): pl.pallas_call(fused_kernel, out_shape=jax.ShapeDtypeStruct((tokens, QUER...]
where the time goes in v2:
time: 51 us; the launch traced here: 50.9 us
  Pallas kernels  48.6 us (95%)
  local copies, waits for them, and re-layouts  2.26 us (4%)
    pallas_call x1, Pallas kernels, on_device_fused(): pl.pallas_call(fused_kernel, out_shape=jax.ShapeDtypeStruct((tokens, QUER...  48.6 us
    unnamed x1, local copies, waits for them, and re-layouts  2.26 us

profile of v2, /device:TPU:23, one launch (start us, length us, event | category | flops | bytes accessed | tf_op | source)
XLA Modules:
  0.0 50.9 jit_solution(9093527693272049664)
XLA Ops:
  0.0 48.6 %shard_map.64 = bf16[512,1024]{1,0:T(8,128)(2,1)} custom-call(s32[1,512]{1,0:T(1,128)} %bitcast.2, s32[1,512]{1,0:T(1,128)} %bitcast.3, bf16[512,1024]{1,0:T(8,128)(2,1)} %events_hbm.1, bf16[1024,1024]{1,0:T(8,128)(2,1)} %wq_hbm.1, bf16[1024,256]{1,0:T(8,128)(2,1)} %wk_hbm.1, bf16[1024,256]{1,0:T(8,128)(2,1)} %wv_hbm.1), custom_call_target="tpu_custom_call" | custom-call | tf_op jit(solution)/shard_map/pallas_call | solution.py:269
  48.6 2.3 %copy.8 = bf16[512,1024]{1,0:T(8,128)(2,1)} copy(bf16[512,1024]{1,0:T(8,128)(2,1)} %shard_map.64) | data formatting | bytes 2097152

commit v3 on v2

--- a/solution.py
+++ b/solution.py
@@ -87,16 +87,6 @@
         info_copy(d).start()
 
     loads[0].wait()
-    rows_sorted[...] = jnp.dot(order, events[...], preferred_element_type=f32).astype(jnp.bfloat16)
-    loads[1].wait()
-    loads[2].wait()
-    keys = jnp.dot(rows_sorted[...], wk[...], preferred_element_type=f32).astype(jnp.bfloat16)
-    values = jnp.dot(rows_sorted[...], wv[...], preferred_element_type=f32).astype(jnp.bfloat16)
-    for h in range(KEY_VALUE_HEADS):
-        cols = slice(h * HEAD_SIZE, (h + 1) * HEAD_SIZE)
-        kv_send[h, :, :, 0:HEAD_SIZE] = keys[:, cols].reshape(n, blk, HEAD_SIZE)
-        kv_send[h, :, :, HEAD_SIZE:] = values[:, cols].reshape(n, blk, HEAD_SIZE)
-
     def kv_copy(j, d, c):
         to_chip = (chip + d) % (n // 2)
         return pltpu.make_async_remote_copy(
@@ -110,13 +100,25 @@
             device_id={"ctx": sibling}, device_id_type=pl.DeviceIdType.MESH,
         )
 
-    @pl.loop(0, n)
-    def _(j):
-        for d in range(1, n // 2):
-            for c in range(2):
-                kv_copy(j, d, c).start()
-        sibling_kv(j).start()
-        kv[j, me] = kv_send[core, j]
+    part = 2 * blk
+    loads[1].wait()
+    loads[2].wait()
+    for p in range(n // 2):
+        here = slice(p * part, (p + 1) * part)
+        rows = jnp.dot(order[here], events[...], preferred_element_type=f32).astype(jnp.bfloat16)
+        rows_sorted[here, :] = rows
+        keys = jnp.dot(rows, wk[...], preferred_element_type=f32).astype(jnp.bfloat16)
+        values = jnp.dot(rows, wv[...], preferred_element_type=f32).astype(jnp.bfloat16)
+        for h in range(KEY_VALUE_HEADS):
+            cols = slice(h * HEAD_SIZE, (h + 1) * HEAD_SIZE)
+            kv_send[h, 2 * p : 2 * p + 2, :, 0:HEAD_SIZE] = keys[:, cols].reshape(2, blk, HEAD_SIZE)
+            kv_send[h, 2 * p : 2 * p + 2, :, HEAD_SIZE:] = values[:, cols].reshape(2, blk, HEAD_SIZE)
+        for j in (2 * p, 2 * p + 1):
+            for d in range(1, n // 2):
+                for c in range(2):
+                    kv_copy(j, d, c).start()
+            sibling_kv(j).start()
+            kv[j, me] = kv_send[core, j]
 
     loads[3].wait()
     for h in range(KEY_VALUE_HEADS):

time: 51 us -> 50.4 us (0.988)
  Pallas kernels: 48.6 us -> 47.9 us
    pallas_call x1, Pallas kernels: 48.6 us -> 47.9 us  [on_device_fused(): pl.pallas_call(fused_kernel, out_shape=jax.ShapeDtypeStruct((tokens, QUER...]
where the time goes in v3:
time: 50.4 us; the launch traced here: 50.2 us
  Pallas kernels  47.9 us (95%)
  local copies, waits for them, and re-layouts  2.26 us (4%)
    pallas_call x1, Pallas kernels, on_device_fused(): pl.pallas_call(fused_kernel, out_shape=jax.ShapeDtypeStruct((tokens, QUER...  47.9 us
    unnamed x1, local copies, waits for them, and re-layouts  2.26 us

profile of v3, /device:TPU:23, one launch (start us, length us, event | category | flops | bytes accessed | tf_op | source)
XLA Modules:
  0.0 50.2 jit_solution(8384710326761606305)
XLA Ops:
  0.0 47.9 %shard_map.64 = bf16[512,1024]{1,0:T(8,128)(2,1)} custom-call(s32[1,512]{1,0:T(1,128)} %bitcast.2, s32[1,512]{1,0:T(1,128)} %bitcast.3, bf16[512,1024]{1,0:T(8,128)(2,1)} %events_hbm.1, bf16[1024,1024]{1,0:T(8,128)(2,1)} %wq_hbm.1, bf16[1024,256]{1,0:T(8,128)(2,1)} %wk_hbm.1, bf16[1024,256]{1,0:T(8,128)(2,1)} %wv_hbm.1), custom_call_target="tpu_custom_call" | custom-call | tf_op jit(solution)/shard_map/pallas_call | solution.py:271
  47.9 2.3 %copy.8 = bf16[512,1024]{1,0:T(8,128)(2,1)} copy(bf16[512,1024]{1,0:T(8,128)(2,1)} %shard_map.64) | data formatting | bytes 2097152
